TPU v7x, 512 devices: a whole 4x8x8 slice. The times are simulated.
512 devices in a mesh: dp: 64 (over z, y), mp: 8 (over x, core).
Axes of the slice: x: 4, y: 8, z: 8, core: 2. Of those that a mesh axis runs over, the one named last changes fastest.
Arguments:
- gradients: float32 [64, 4, 128, 8192], P('dp', None, 'mp'), may hold values from -16 to 16
- weights: float32 [4, 128, 8192], P(None, 'mp', 'dp'), may hold values from -40 to 40
- first_moment: float32 [4, 128, 8192], P(None, 'mp', 'dp'), may hold values from -0.6 to 0.6
- second_moment: float32 [4, 128, 8192], P(None, 'mp', 'dp'), may hold values from 0.001 to 0.1
- learn_rate: float32 [4], replicated, may hold values from 0.1 to 0.5
- weight_decay: float32 [4], replicated, may hold values from 0.1 to 1
Outputs:
- new_weights: float32 [4, 128, 8192], P(None, 'mp')
- new_first: float32 [4, 128, 8192], P(None, 'mp', 'dp')
- new_second: float32 [4, 128, 8192], P(None, 'mp', 'dp')
- trust_ratio: float32 [4], replicated
All inputs are finite; a program needn't handle non-finite values.
Results may differ from a plain program's by a relative error of at most 0.000062.
Values sent between devices are 32-bit elements; how exact they have to be, the bound alone decides.
A program may use at most 64 MiB of HBM per device.

v0:
```python
import jax
import jax.numpy as jnp
from jax import lax
from jax.sharding import PartitionSpec as P

STEP = 10


def cut_along(shard, dim, length):
    before, after = (shard.shape[:dim], shard.shape[dim + 1 :])
    return jnp.moveaxis(shard.reshape(*before, length, -1, *after), dim, 0)


def sent_and_summed(shard, axis, dim):
    parts = cut_along(shard, dim, lax.axis_size(axis))
    arrived = lax.all_to_all(parts, axis, split_axis=0, concat_axis=0, tiled=True)
    return arrived.sum(axis=0)


def in_one_piece(arrays, axis, dim, along):
    ends, at = ([], 0)
    for a in arrays[:-1]:
        at += a.shape[along]
        ends.append(at)
    both = jnp.concatenate(arrays, axis=along)
    return tuple(jnp.split(lax.all_gather(both, axis, axis=dim, tiled=True), ends, axis=along))


def from_everyone(shard, axis):
    length = lax.axis_size(axis)
    return lax.all_to_all(
        jnp.broadcast_to(shard[None], (length, *shard.shape)), axis, 0, 0, tiled=True
    )


def over_copies(shard, axis):
    everything = from_everyone(shard, axis)
    return jnp.sum(everything, axis=0)


def together(arrays, axis):
    ends = [0]
    for a in arrays:
        ends.append(ends[-1] + a.size)
    so_far = over_copies(jnp.concatenate([a.ravel() for a in arrays]), axis)
    return tuple((so_far[b:e].reshape(a.shape) for a, b, e in zip(arrays, ends, ends[1:])))


def shards(gradients, weights, first_moment, second_moment, learn_rate, weight_decay):
    replicas = lax.axis_size("dp")
    summed = sent_and_summed(gradients, "dp", 3)[0] * (1.0 / replicas)
    new_first = 0.9 * first_moment + 0.1 * summed
    new_second = 0.999 * second_moment + 0.001 * summed * summed
    first_fix = 1.0 - 0.9**STEP
    second_fix = 1.0 - 0.999**STEP
    update = (
        new_first / first_fix / (jnp.sqrt(new_second / second_fix) + 1e-06)
        + weight_decay[:, None, None] * weights
    )
    whole_weights, whole_update = in_one_piece((weights, update), "dp", 2, 0)
    weight_sq, update_sq = together(
        (
            jnp.sum(whole_weights * whole_weights, axis=(1, 2)),
            jnp.sum(whole_update * whole_update, axis=(1, 2)),
        ),
        "mp",
    )
    trust_ratio = jnp.sqrt(weight_sq) / (jnp.sqrt(update_sq) + 1e-06)
    new_weights = whole_weights - (learn_rate * trust_ratio)[:, None, None] * whole_update
    return (new_weights, new_first, new_second, trust_ratio)


def solution(mesh):
    in_specs = (
        P("dp", None, "mp", None),
        P(None, "mp", "dp"),
        P(None, "mp", "dp"),
        P(None, "mp", "dp"),
        P(),
        P(),
    )
    out_specs = (P(None, "mp", None), P(None, "mp", "dp"), P(None, "mp", "dp"), P())
    return jax.shard_map(shards, mesh=mesh, in_specs=in_specs, out_specs=out_specs, check_vma=False)
```

profile of v0, /device:TPU:1, one launch (start us, length us, event | category | flops | bytes accessed | tf_op | source)
XLA Modules:
  0.0 194.2 jit_solution(12257674370459160557)
XLA Ops:
  7.2 0.0 all-gather.2.cloned.1.call-start
  7.2 2.0 %copy.14 = f32[8,8,64,128]{3,2,1,0:T(8,128)S(1)} copy(f32[8,8,64,128]{3,1,2,0:T(8,128)} %bitcast.10) | data formatting | bytes 4194304
  9.2 1.2 copy.12
  10.4 66.2 %all_to_all.11 = f32[64,1,4,16,128]{4,3,2,1,0:T(8,128)S(1)} all-to-all(f32[64,1,4,16,128]{4,3,2,1,0:T(8,128)S(1)} %copy.12), channel_id=1, replica_groups=mesh['dp'=64,'mp'=8] {'dp'}, dimensions={0} | all-to-all | bytes 4194304 | tf_op jit(solution)/shard_map/all_to_all | solution.py:16
  76.6 0.0 copy-start
  76.6 0.0 copy-start.1
  76.7 0.0 copy-start.2
  76.7 0.0 copy-start.3
  76.7 0.1 reduce_sum.36
  76.8 0.6 copy-done
  77.4 0.0 copy-done.1
  77.4 0.0 copy-done.2
  77.4 0.0 copy-done.3
  77.4 0.6 multiply_add_fusion
  78.1 0.6 pad_maximum_fusion
  78.7 0.0 all-gather.2.cloned.1.call-update
  78.7 0.0 copy-start.4
  78.8 87.5 %all-gather.2.cloned.1.call-done = f32[8,16,8192]{2,1,0:T(8,128)} async-done(((f32[8,16,128]{2,1,0:T(8,128)}), f32[8,16,8192]{2,1,0:T(8,128)}) %all-gather.2.cloned.1.call-update) | async-done | bytes 4194320 | tf_op jit(solution)/shard_map/all_gather | solution.py:26
  166.3 2.7 %multiply_reduce_fusion.1 = (f32[4]{0:T(128)S(1)}, f32[4]{0:T(128)S(1)}) fusion(f32[8,16,8192]{2,1,0:T(8,128)} %all-gather.2.cloned.1.call-done), kind=kLoop, calls=%fused_computation.2 | loop fusion | flops 2097144 | bytes 4194336 | tf_op jit(solution)/shard_map/reduce_sum | solution.py:63
  168.9 0.1 pad_maximum_fusion.1
  169.0 13.9 %all_to_all.12 = f32[8,1,8]{2,1,0:T(1,128)S(1)} all-to-all(f32[8,1,8]{2,1,0:T(1,128)S(1)} %broadcast_in_dim.2), channel_id=1, replica_groups=mesh['dp'=64,'mp'=8] {'mp'}, dimensions={0} | all-to-all | bytes 512 | tf_op jit(solution)/shard_map/all_to_all | solution.py:31
  183.0 0.0 copy-done.4
  183.0 0.6 fusion
  183.6 3.8 %multiply_subtract_fusion = f32[4,16,8192]{2,1,0:T(8,128)} fusion(f32[8,16,8192]{2,1,0:T(8,128)} %all-gather.2.cloned.1.call-done, f32[4]{0:T(128)S(1)} %get-tuple-element.6), kind=kLoop, calls=%fused_computation | loop fusion | flops 1048576 | bytes 6291472 | tf_op jit(solution)/shard_map/sub | solution.py:69
  (2 shorter events, 0.0 us)
Async XLA Ops:
  7.2 159.1 %all-gather.2.cloned.1.call-start = ((), (), s32[]{:S(2)}) async-start(), calls=%async_computation.2 | async-start | bytes 4259840 | tf_op jit(solution)/shard_map/all_gather | solution.py:26
  76.6 0.8 copy-start
  76.6 0.8 copy-start.1
  76.7 0.8 copy-start.2
  76.7 0.8 copy-start.3
  78.7 104.2 %copy-start.4 = (f32[4]{0:T(128)S(1)}, f32[4]{0:T(128)}, u32[]{:S(2)}) copy-start(f32[4]{0:T(128)} %param.10) | copy-start | bytes 52
Sparse Core Ops, SparseCore 0:
  78.9 87.3 all-gather.1
where the time goes:
time: 194 us
  waiting for transfers between devices  87.5 us (45%)
  blocking collectives  80.2 us (41%)
  between operations  14.1 us (7%)
  other arithmetic  8.58 us (4%)
  local copies, waits for them, and re-layouts  3.84 us (2%)
    all_gather x1, waiting for transfers between devices, in_one_piece(): lax.all_gather(both, axis, axis=dim, tiled=True)  87.5 us
    all_to_all x1, blocking collectives, sent_and_summed(): lax.all_to_all(parts, axis, split_axis=0, concat_axis=0, tiled=True)  66.2 us
    all_to_all x1, blocking collectives, from_everyone(): lax.all_to_all(jnp.broadcast_to(shard[None], (length, *shard.shape)), axi...  13.9 us
  transfers between devices with their start and end apart: 1, of which 1 were waited for; matrix products, arithmetic and copies ran while one was open for 0% of the time, Pallas kernels for 0%

commit v1 on v0

v1 whole, which is shorter than its diff:
```python
import functools

import jax
import jax.numpy as jnp
from jax import lax
from jax.experimental import pallas as pl
from jax.experimental.pallas import tpu as pltpu
from jax.sharding import PartitionSpec as P

STEP = 10
NT = 4
SIDE = 8
F32 = jnp.float32
MESH = pl.DeviceIdType.MESH

LATE = (0, 1, 2, 3)


def order():
    steps = []
    for s in range(1, 5):
        steps += [("reduce", t, s) for t in range(NT)]
        steps += [("near_weights", s)]
    for t in range(NT):
        steps += [("spread", t)]
    steps += [("near_weights", 5)]
    for t in range(NT):
        steps += [("update", t)]
    for t in range(NT):
        steps += [("squares", t)]
    steps += [("total", 0), ("total", 1), ("total", 2)]
    for s in range(1, 5):
        steps += [("late", t, s) for t in range(NT)]
    for t in range(NT):
        steps += [("finish", t)]
    return steps


def length(t, h, d):
    return 4 if (t + h + d) % 2 == 0 else 3


def kernel(
    g_hbm, w_hbm, m_hbm, v_hbm, lr, wd,
    out_hbm, nf_hbm, ns_hbm, tr_out,
    g, w, m, v, nf, ns, ring, own, cross, u1, w1, out, sq_a, sq_b, sq_m, squares,
    load_g, load_s, ring_s, ring_r, cross_s, cross_r, u1_s, u1_r, w1_s, w1_r, sq_s, sq_r, ag_s, ag_r, out_s,
):
    dp, mp = lax.axis_index("dp"), lax.axis_index("mp")
    z, y = dp // SIDE, dp % SIDE

    def mod(i):
        return lax.rem(i + 2 * SIDE, SIDE)

    def ring_peer(h, k):
        return (z * SIDE + mod(y + k), mp) if h == 0 else (mod(z + k) * SIDE + y, mp)

    def cross_peer(h, k):
        return ring_peer(1 - h, k)

    def ring_at(h):
        return y if h == 0 else z

    def cross_at(h):
        return z if h == 0 else y

    def chunk(ref, t, h, r):
        return ref.at[t, 0, :, r] if h == 0 else ref.at[t, 1, r]

    def tile(ref, t, h, r, c):
        return ref.at[t, 0, c, r] if h == 0 else ref.at[t, 1, r, c]

    def send(src, dst, ss, rs, to):
        copy = pltpu.make_async_remote_copy(
            src_ref=src, dst_ref=dst, send_sem=ss, recv_sem=rs, device_id=to, device_id_type=MESH
        )
        copy.start()

    def arrived(ref, sem):
        pltpu.make_async_copy(ref, ref, sem).wait()

    loads = []
    for t in range(NT):
        for h in range(2):
            loads.append(pltpu.make_async_copy(g_hbm.at[t, h], g.at[t, h], load_g.at[t, h]))
    small = [
        pltpu.make_async_copy(a, b, load_s.at[i])
        for i, (a, b) in enumerate(((w_hbm, w), (m_hbm, m), (v_hbm, v)))
    ]
    for c in loads + small:
        c.start()

    barrier = pltpu.get_barrier_semaphore()
    near = [ring_peer(h, k) for h in range(2) for k in (1, -1)] + [(dp, mod(mp + k)) for k in range(1, SIDE)]
    for peer in near:
        pl.semaphore_signal(barrier, inc=1, device_id=peer, device_id_type=MESH)
    pl.semaphore_wait(barrier, len(near))

    first_fix = 1.0 - 0.9**STEP
    second_fix = 1.0 - 0.999**STEP
    scale = {}

    def reduce(t, s):
        for h in range(2):
            if s == 1:
                loads[2 * t + h].wait()
            for d, sign in enumerate((1, -1)):
                n = length(t, h, d)
                if s > n:
                    continue
                mine = chunk(g, t, h, mod(ring_at(h) + sign * (n - s + 1)))
                if s == 1:
                    src = mine
                else:
                    src = ring.at[t, h, d, s - 2]
                    arrived(src, ring_r.at[t, h, d, s - 2])
                    src[...] += mine[...]
                send(src, ring.at[t, h, d, s - 1], ring_s, ring_r.at[t, h, d, s - 1], ring_peer(h, sign))

    def near_weights(s):
        if s == 1:
            for c in small:
                c.wait()
            for h in range(2):
                w1[h, cross_at(h)] = w[:, h]
        for h in range(2):
            for d, sign in enumerate((1, -1)):
                n = length(0, h, d)
                if 1 < s <= n + 1:
                    at = w1.at[h, mod(cross_at(h) - sign * (s - 1))]
                    arrived(at, w1_r.at[h, d, s - 2])
                if s <= n:
                    at = w1.at[h, mod(cross_at(h) - sign * (s - 1))]
                    send(at, at, w1_s, w1_r.at[h, d, s - 1], cross_peer(h, sign))

    def spread(t):
        for h in range(2):
            total = chunk(g, t, h, ring_at(h))[...]
            for d in range(2):
                last = length(t, h, d) - 1
                arrived(ring.at[t, h, d, last], ring_r.at[t, h, d, last])
                total += ring[t, h, d, last]
            own[t, h] = total
        for h in range(2):
            for k in (4, 3, 5, 2, 6, 1, 7):
                send(
                    own.at[t, h, mod(cross_at(h) + k)], cross.at[t, h, cross_at(h)],
                    cross_s, cross_r.at[t, h], cross_peer(h, k),
                )

    def update(t):
        for h in range(2):
            cross[t, h, cross_at(h)] = own[t, h, cross_at(h)]
            arrived(cross.at[t, h, 0:7], cross_r.at[t, h])
            summed = jnp.sum(cross[t, h], axis=0) * (1.0 / (SIDE * SIDE))
            new_first = 0.9 * m[t, h] + 0.1 * summed
            new_second = 0.999 * v[t, h] + 0.001 * summed * summed
            nf[t, h] = new_first
            ns[t, h] = new_second
            u1[t, h, cross_at(h)] = (
                new_first / first_fix / (jnp.sqrt(new_second / second_fix) + 1e-06) + wd[t] * w[t, h]
            )
            at = u1.at[t, h, cross_at(h)]
            for k in (4, 3, 5, 2, 6, 1, 7):
                send(at, at, u1_s, u1_r.at[t, h], cross_peer(h, k))

    def squared(a):
        return jnp.sum(jnp.sum(a * a, axis=0), axis=0, keepdims=True)

    def squares_of(t):
        for h in range(2):
            arrived(u1.at[t, h, 0:7], u1_r.at[t, h])
            squares[h, t : t + 1] = squared(w1[h, :, t])
            squares[h, NT + t : NT + t + 1] = squared(u1[t, h])

    def total(stage):
        if stage == 0:
            for h, slots in enumerate((sq_a, sq_b)):
                slots[ring_at(h)] = squares[h]
                for k in (4, 3, 5, 2, 6, 1, 7):
                    send(squares.at[h], slots.at[ring_at(h)], sq_s, sq_r.at[h], ring_peer(h, k))
        if stage == 1:
            for h, slots in enumerate((sq_a, sq_b)):
                arrived(slots.at[0:7], sq_r.at[h])
            squares[2] = jnp.sum(sq_a[...], axis=0) + jnp.sum(sq_b[...], axis=0)
            sq_m[mp] = squares[2]
            for k in (4, 3, 5, 2, 6, 1, 7):
                send(squares.at[2], sq_m.at[mp], sq_s, sq_r.at[2], (dp, mod(mp + k)))
        if stage == 2:
            arrived(sq_m.at[0:7], sq_r.at[2])
            both = jnp.sum(sq_m[...], axis=0)
            for t in range(NT):
                weight_sq = jnp.sum(both[t : t + 1], axis=1, keepdims=True)
                update_sq = jnp.sum(both[NT + t : NT + t + 1], axis=1, keepdims=True)
                ratio = jnp.sqrt(weight_sq) / (jnp.sqrt(update_sq) + 1e-06)
                tr_out[t] = jnp.max(ratio)
                scale[t] = lr[t] * ratio

    def around(ref, t, s, sems, sem):
        for h in range(2):
            for d, sign in enumerate((1, -1)):
                n = length(t, h, d)
                at = chunk(ref, t, h, mod(ring_at(h) - sign * (s - 1)))
                if 1 < s <= n + 1:
                    arrived(at, sems.at[t, h, d, s - 2])
                if s <= n:
                    send(at, at, sem, sems.at[t, h, d, s - 1], ring_peer(h, sign))

    def late(t, s):
        if s == 1:
            for h in range(2):
                chunk(out, t, h, ring_at(h))[...] = w1[h, :, t] - scale[t][None] * u1[t, h]
        around(out, t, s, ag_r, ag_s)

    def finish(t):
        around(out, t, 5, ag_r, ag_s)
        pltpu.make_async_copy(out.at[t], out_hbm.at[t], out_s.at[t]).start()

    acts = {
        "reduce": reduce, "near_weights": near_weights, "spread": spread, "update": update,
        "squares": squares_of, "total": total, "late": late, "finish": finish,
    }
    for name, *args in order():
        acts[name](*args)
        if name == "update" and args[0] == NT - 1:
            outs = [
                pltpu.make_async_copy(nf, nf_hbm, out_s.at[NT]),
                pltpu.make_async_copy(ns, ns_hbm, out_s.at[NT + 1]),
            ]
            for c in outs:
                c.start()

    arrived(g.at[:, :, 0:7], ring_s)
    arrived(g.at[:, :, 0:7], ag_s)
    arrived(g.at[0, 0, 0:7], cross_s)
    arrived(g.at[0, 0, 0:7], u1_s)
    arrived(g.at[0, 0, 0:7], w1_s)
    arrived(g.at[0, 0:1, 0:3, 0:7], sq_s)
    for t in range(NT):
        pltpu.make_async_copy(out.at[t], out_hbm.at[t], out_s.at[t]).wait()
    for c in outs:
        c.wait()


def shards(gradients, weights, first_moment, second_moment, learn_rate, weight_decay):
    tiles = (NT, 2, SIDE, SIDE, 8, 128)
    mine = (NT, 2, 8, 128)
    g = gradients.reshape(NT, 2, 8, SIDE, SIDE, 128).transpose(0, 1, 3, 4, 2, 5)
    dma = pltpu.SemaphoreType.DMA
    any_space = pl.BlockSpec(memory_space=pl.ANY)
    smem = pl.BlockSpec(memory_space=pltpu.SMEM)
    out, nf, ns, tr = pl.pallas_call(
        kernel,
        out_shape=(
            jax.ShapeDtypeStruct(tiles, F32),
            jax.ShapeDtypeStruct(mine, F32),
            jax.ShapeDtypeStruct(mine, F32),
            jax.ShapeDtypeStruct((NT,), F32),
        ),
        in_specs=[any_space] * 4 + [smem] * 2,
        out_specs=(any_space, any_space, any_space, smem),
        scratch_shapes=[
            pltpu.VMEM(tiles, F32),
            *[pltpu.VMEM(mine, F32)] * 5,
            pltpu.VMEM((NT, 2, 2, 4, SIDE, 8, 128), F32),
            pltpu.VMEM((NT, 2, SIDE, 8, 128), F32),
            pltpu.VMEM((NT, 2, SIDE, 8, 128), F32),
            pltpu.VMEM((NT, 2, SIDE, 8, 128), F32),
            pltpu.VMEM((2, SIDE, NT, 8, 128), F32),
            pltpu.VMEM(tiles, F32),
            *[pltpu.VMEM((SIDE, 8, 128), F32)] * 3,
            pltpu.VMEM((3, 8, 128), F32),
            dma((NT, 2)), dma((3,)),
            dma, dma((NT, 2, 2, 4)),
            dma, dma((NT, 2)),
            dma, dma((NT, 2)),
            dma, dma((2, 2, 4)),
            dma, dma((3,)),
            dma, dma((NT, 2, 2, 4)),
            dma((NT + 2,)),
        ],
        compiler_params=pltpu.CompilerParams(
            collective_id=0, has_side_effects=True, vmem_limit_bytes=48 * 2**20
        ),
        name="lamb",
    )(
        g, *(a.reshape(mine) for a in (weights, first_moment, second_moment)), learn_rate, weight_decay
    )
    new_weights = out.transpose(0, 1, 4, 2, 3, 5).reshape(NT, 16, SIDE * SIDE * 128)
    return new_weights, nf.reshape(NT, 16, 128), ns.reshape(NT, 16, 128), tr


def solution(mesh):
    in_specs = (
        P("dp", None, "mp", None),
        P(None, "mp", "dp"),
        P(None, "mp", "dp"),
        P(None, "mp", "dp"),
        P(),
        P(),
    )
    out_specs = (P(None, "mp", None), P(None, "mp", "dp"), P(None, "mp", "dp"), P())
    return jax.shard_map(shards, mesh=mesh, in_specs=in_specs, out_specs=out_specs, check_vma=False)
```

time: 194 us -> 75.6 us (0.39)
  the two profiles are of different devices: /device:TPU:1 before, /device:TPU:2 now
where the time goes in v1:
time: 75.6 us; the launch traced here: 75.2 us
  Pallas kernels  66.4 us (88%)
  local copies, waits for them, and re-layouts  8.23 us (11%)
    pallas_call x1, Pallas kernels, shards(): pl.pallas_call(kernel, out_shape=(jax.ShapeDtypeStruct(tiles, F32), jax.S...  66.4 us
    unnamed x16, local copies, waits for them, and re-layouts  8.23 us

profile of v1, /device:TPU:2, one launch (start us, length us, event | category | flops | bytes accessed | tf_op | source)
XLA Modules:
  0.0 75.2 jit_solution(8963691731836413254)
XLA Ops:
  0.6 0.0 copy-start
  0.6 1.6 %copy-done = f32[1,4,16,8192]{3,2,1,0:T(8,128)S(1)} copy-done((f32[1,4,16,8192]{3,2,1,0:T(8,128)S(1)}, f32[1,4,16,8192]{3,2,1,0:T(8,128)}, u32[]{:S(2)}) %copy-start) | copy-done | bytes 2097176
  2.2 0.0 copy-start.1
  2.2 0.8 %copy-done.1 = f32[4,16,128]{2,1,0:T(8,128)S(1)} copy-done((f32[4,16,128]{2,1,0:T(8,128)S(1)}, f32[4,16,128]{2,1,0:T(8,128)}, u32[]{:S(2)}) %copy-start.1) | copy-done | bytes 32792
  3.0 0.0 copy-start.2
  3.0 0.8 %copy-done.2 = f32[4,16,128]{2,1,0:T(8,128)S(1)} copy-done((f32[4,16,128]{2,1,0:T(8,128)S(1)}, f32[4,16,128]{2,1,0:T(8,128)}, u32[]{:S(2)}) %copy-start.2) | copy-done | bytes 32792
  3.7 0.0 copy-start.3
  3.7 0.8 %copy-done.3 = f32[4,16,128]{2,1,0:T(8,128)S(1)} copy-done((f32[4,16,128]{2,1,0:T(8,128)S(1)}, f32[4,16,128]{2,1,0:T(8,128)}, u32[]{:S(2)}) %copy-start.3) | copy-done | bytes 32792
  4.5 0.0 copy-start.4
  4.5 0.7 copy-done.4
  5.2 0.0 copy-start.5
  5.2 0.7 copy-done.5
  5.8 66.4 %lamb.1 = (f32[4,2,8,8,8,128]{5,4,3,2,1,0:T(8,128)S(1)}, f32[4,2,8,128]{3,2,1,0:T(8,128)S(1)}, f32[4,2,8,128]{3,2,1,0:T(8,128)S(1)}, f32[4]{0:T(128)S(1)}) custom-call(f32[4,2,8,8,8,128]{5,4,3,2,1,0:T(8,128)S(1)} %bitcast.11, f32[4,2,8,128]{3,2,1,0:T(8,128)S(1)} %bitcast.13, f32[4,2,8,128]{3,2,1,0:T(8,128)S(1)} %bitcast.14, f32[4,2,8,128]{3,2,1,0:T(8,128)S(1)} %bitcast.15, ...), custom_call_target="tpu_custom_call" | custom-call | tf_op jit(solution)/shard_map/lamb/pallas_call | solution.py:252
  72.2 1.3 %copy.14 = f32[4,16,8192]{2,1,0:T(8,128)} copy(f32[4,16,8192]{2,1,0:T(8,128)S(1)} %bitcast.12) | data formatting | bytes 4194304
  73.5 0.6 copy.15
  74.1 0.6 copy.16
  74.7 0.5 copy.17
Async XLA Ops:
  0.6 1.6 %copy-start = (f32[1,4,16,8192]{3,2,1,0:T(8,128)S(1)}, f32[1,4,16,8192]{3,2,1,0:T(8,128)}, u32[]{:S(2)}) copy-start(f32[1,4,16,8192]{3,2,1,0:T(8,128)} %param.6) | copy-start | bytes 6291460
  2.2 0.8 %copy-start.1 = (f32[4,16,128]{2,1,0:T(8,128)S(1)}, f32[4,16,128]{2,1,0:T(8,128)}, u32[]{:S(2)}) copy-start(f32[4,16,128]{2,1,0:T(8,128)} %param.7) | copy-start | bytes 98308
  3.0 0.8 %copy-start.2 = (f32[4,16,128]{2,1,0:T(8,128)S(1)}, f32[4,16,128]{2,1,0:T(8,128)}, u32[]{:S(2)}) copy-start(f32[4,16,128]{2,1,0:T(8,128)} %param.8) | copy-start | bytes 98308
  3.7 0.8 %copy-start.3 = (f32[4,16,128]{2,1,0:T(8,128)S(1)}, f32[4,16,128]{2,1,0:T(8,128)}, u32[]{:S(2)}) copy-start(f32[4,16,128]{2,1,0:T(8,128)} %param.9) | copy-start | bytes 98308
  4.5 0.7 copy-start.4
  5.2 0.7 copy-start.5

commit v2 on v1

--- a/solution.py
+++ b/solution.py
@@ -13,27 +13,33 @@
 F32 = jnp.float32
 MESH = pl.DeviceIdType.MESH
 
-LATE = (0, 1, 2, 3)
-
 
 def order():
-    steps = []
+    every = range(NT)
+    steps = [("near_weights", 1)]
     for s in range(1, 5):
-        steps += [("reduce", t, s) for t in range(NT)]
-        steps += [("near_weights", s)]
-    for t in range(NT):
-        steps += [("spread", t)]
-    steps += [("near_weights", 5)]
-    for t in range(NT):
-        steps += [("update", t)]
-    for t in range(NT):
-        steps += [("squares", t)]
-    steps += [("total", 0), ("total", 1), ("total", 2)]
-    for s in range(1, 5):
-        steps += [("late", t, s) for t in range(NT)]
-    for t in range(NT):
-        steps += [("finish", t)]
-    return steps
+        steps += [("reduce", t, s) for t in every] + [("near_weights", s + 1)] * (s < 4)
+    steps += [("spread", t) for t in every] + [("near_weights", 5)]
+    steps += [("weights", t, 1) for t in every]
+    steps += [("update", t) for t in every]
+    steps += [("weights", t, 2) for t in every]
+    for t in every:
+        steps += [("near_updates", t), ("updates", t, 1)]
+    steps += [("squares", t) for t in every] + [("total", 0)]
+    steps += [("updates", t, 2) for t in every]
+    steps += [("weights", t, 3) for t in every] + [("total", 1)]
+    steps += [("updates", t, 3) for t in every]
+    steps += [("weights", t, 4) for t in every] + [("total", 2)]
+    steps += [("updates", t, 4) for t in every]
+    return steps + [("last", t) for t in every]
+
+
+TO_OWNER = ((1, 4, 3), (1, -3, -2), (2, 3, 2), (2, -2, -1), (3, 2, 1), (3, -1, 0), (4, 1, 0))
+FROM_OWNER = ((1, 0, 1), (1, 0, -1), (2, 1, 2), (2, -1, -2), (3, 2, 3), (3, -2, -3), (4, 3, 4))
+
+
+def side(t, h):
+    return 1 if (t + h) % 2 == 0 else -1
 
 
 def length(t, h, d):
@@ -41,10 +47,10 @@
 
 
 def kernel(
-    g_hbm, w_hbm, m_hbm, v_hbm, lr, wd,
-    out_hbm, nf_hbm, ns_hbm, tr_out,
-    g, w, m, v, nf, ns, ring, own, cross, u1, w1, out, sq_a, sq_b, sq_m, squares,
-    load_g, load_s, ring_s, ring_r, cross_s, cross_r, u1_s, u1_r, w1_s, w1_r, sq_s, sq_r, ag_s, ag_r, out_s,
+    g_hbm, w_hbm, m_hbm, v_hbm, lr_hbm, wd_hbm,
+    all_w, all_u, scale_out, nf_out, ns_out, tr_out,
+    g, w, m, v, nf, ns, lr, wd, ring, own, cross, u1, w1, w_own, scale, sq_a, sq_b, sq_m, squares,
+    load_g, load_s, ring_s, ring_r, cross_s, cross_r, u1_s, u1_r, w1_s, w1_r, sq_s, sq_r, aw_s, aw_r, au_s, au_r, out_s, res_s,
 ):
     dp, mp = lax.axis_index("dp"), lax.axis_index("mp")
     z, y = dp // SIDE, dp % SIDE
@@ -85,7 +91,7 @@
             loads.append(pltpu.make_async_copy(g_hbm.at[t, h], g.at[t, h], load_g.at[t, h]))
     small = [
         pltpu.make_async_copy(a, b, load_s.at[i])
-        for i, (a, b) in enumerate(((w_hbm, w), (m_hbm, m), (v_hbm, v)))
+        for i, (a, b) in enumerate(((w_hbm, w), (m_hbm, m), (v_hbm, v), (lr_hbm, lr), (wd_hbm, wd)))
     ]
     for c in loads + small:
         c.start()
@@ -98,24 +104,37 @@
 
     first_fix = 1.0 - 0.9**STEP
     second_fix = 1.0 - 0.999**STEP
-    scale = {}
+    held, seen = [], set()
+
+    def keep(src, dst, sem):
+        held.append(pltpu.make_async_copy(src, dst, sem))
+        held[-1].start()
+
+    def block_sum(t, h, at):
+        mine = chunk(g, t, h, mod(ring_at(h) - side(t, h) * at))
+        parts = [ring.at[t, h, a % SIDE] for _, a, b in TO_OWNER if b == at]
+        for _, a, b in TO_OWNER:
+            if b == at:
+                arrived(ring.at[t, h, a % SIDE], ring_r.at[t, h, a % SIDE])
+        return mine, parts
 
     def reduce(t, s):
         for h in range(2):
             if s == 1:
                 loads[2 * t + h].wait()
-            for d, sign in enumerate((1, -1)):
-                n = length(t, h, d)
-                if s > n:
-                    continue
-                mine = chunk(g, t, h, mod(ring_at(h) + sign * (n - s + 1)))
-                if s == 1:
-                    src = mine
-                else:
-                    src = ring.at[t, h, d, s - 2]
-                    arrived(src, ring_r.at[t, h, d, s - 2])
-                    src[...] += mine[...]
-                send(src, ring.at[t, h, d, s - 1], ring_s, ring_r.at[t, h, d, s - 1], ring_peer(h, sign))
+            for step, a, b in TO_OWNER:
+                if step == s:
+                    src, parts = block_sum(t, h, a)
+                    if parts:
+                        total = src[...]
+                        for part in parts:
+                            total += part[...]
+                        src = parts[0]
+                        src[...] = total
+                    send(
+                        src, ring.at[t, h, a % SIDE], ring_s, ring_r.at[t, h, a % SIDE],
+                        ring_peer(h, side(t, h) * (b - a)),
+                    )
 
     def near_weights(s):
         if s == 1:
@@ -135,11 +154,10 @@
 
     def spread(t):
         for h in range(2):
-            total = chunk(g, t, h, ring_at(h))[...]
-            for d in range(2):
-                last = length(t, h, d) - 1
-                arrived(ring.at[t, h, d, last], ring_r.at[t, h, d, last])
-                total += ring[t, h, d, last]
+            src, parts = block_sum(t, h, 0)
+            total = src[...]
+            for part in parts:
+                total += part[...]
             own[t, h] = total
         for h in range(2):
             for k in (4, 3, 5, 2, 6, 1, 7):
@@ -167,9 +185,12 @@
     def squared(a):
         return jnp.sum(jnp.sum(a * a, axis=0), axis=0, keepdims=True)
 
+    def near_updates(t):
+        for h in range(2):
+            arrived(u1.at[t, h, 0:7], u1_r.at[t, h])
+
     def squares_of(t):
         for h in range(2):
-            arrived(u1.at[t, h, 0:7], u1_r.at[t, h])
             squares[h, t : t + 1] = squared(w1[h, :, t])
             squares[h, NT + t : NT + t + 1] = squared(u1[t, h])
 
@@ -194,51 +215,79 @@
                 update_sq = jnp.sum(both[NT + t : NT + t + 1], axis=1, keepdims=True)
                 ratio = jnp.sqrt(weight_sq) / (jnp.sqrt(update_sq) + 1e-06)
                 tr_out[t] = jnp.max(ratio)
-                scale[t] = lr[t] * ratio
-
-    def around(ref, t, s, sems, sem):
-        for h in range(2):
-            for d, sign in enumerate((1, -1)):
-                n = length(t, h, d)
-                at = chunk(ref, t, h, mod(ring_at(h) - sign * (s - 1)))
-                if 1 < s <= n + 1:
-                    arrived(at, sems.at[t, h, d, s - 2])
-                if s <= n:
-                    send(at, at, sem, sems.at[t, h, d, s - 1], ring_peer(h, sign))
-
-    def late(t, s):
+                scale[t : t + 1] = jnp.broadcast_to(lr[t] * ratio, (1, 128))
+            keep(scale, scale_out, res_s.at[2])
+
+    def around(first, ref, t, s, sems, sem):
+        for h in range(2):
+            for step, a, b in FROM_OWNER:
+                if step == s:
+                    at = chunk(ref, t, h, mod(ring_at(h) - side(t, h) * a))
+                    if a:
+                        landed(ref, t, h, a, sems)
+                    send(
+                        at if a else first.at[t, h], at, sem, sems.at[t, h, b % SIDE],
+                        ring_peer(h, side(t, h) * (b - a)),
+                    )
+
+    def landed(ref, t, h, a, sems):
+        if (ref is all_w, t, h, a) not in seen:
+            seen.add((ref is all_w, t, h, a))
+            arrived(chunk(ref, t, h, mod(ring_at(h) - side(t, h) * a)), sems.at[t, h, a % SIDE])
+
+    def last(t):
+        for h in range(2):
+            for a in (1, -1, 2, -2, 3, -3, 4):
+                landed(all_w, t, h, a, aw_r)
+                landed(all_u, t, h, a, au_r)
+
+    def weights(t, s):
         if s == 1:
             for h in range(2):
-                chunk(out, t, h, ring_at(h))[...] = w1[h, :, t] - scale[t][None] * u1[t, h]
-        around(out, t, s, ag_r, ag_s)
-
-    def finish(t):
-        around(out, t, 5, ag_r, ag_s)
-        pltpu.make_async_copy(out.at[t], out_hbm.at[t], out_s.at[t]).start()
+                w_own[t, h] = w1[h, :, t]
+                keep(w_own.at[t, h], chunk(all_w, t, h, ring_at(h)), out_s.at[0, t, h])
+        around(w_own, all_w, t, s, aw_r, aw_s)
+
+    def updates(t, s):
+        around(u1, all_u, t, s, au_r, au_s)
+        if s == 1:
+            for h in range(2):
+                keep(u1.at[t, h], chunk(all_u, t, h, ring_at(h)), out_s.at[1, t, h])
 
     acts = {
         "reduce": reduce, "near_weights": near_weights, "spread": spread, "update": update,
-        "squares": squares_of, "total": total, "late": late, "finish": finish,
+        "near_updates": near_updates, "squares": squares_of, "total": total, "weights": weights, "updates": updates, "last": last,
     }
     for name, *args in order():
         acts[name](*args)
         if name == "update" and args[0] == NT - 1:
-            outs = [
-                pltpu.make_async_copy(nf, nf_hbm, out_s.at[NT]),
-                pltpu.make_async_copy(ns, ns_hbm, out_s.at[NT + 1]),
-            ]
-            for c in outs:
-                c.start()
+            keep(nf, nf_out, res_s.at[0])
+            keep(ns, ns_out, res_s.at[1])
 
     arrived(g.at[:, :, 0:7], ring_s)
-    arrived(g.at[:, :, 0:7], ag_s)
+    arrived(g.at[:, :, 0:7], aw_s)
+    arrived(g.at[:, :, 0:7], au_s)
     arrived(g.at[0, 0, 0:7], cross_s)
     arrived(g.at[0, 0, 0:7], u1_s)
     arrived(g.at[0, 0, 0:7], w1_s)
     arrived(g.at[0, 0:1, 0:3, 0:7], sq_s)
+    for c in held:
+        c.wait()
+
+
+def results(all_w, all_u, scale, nf, ns, tr, new_out, nf_out, ns_out, tr_out, new, sem, sem_new):
+    copies = [
+        pltpu.make_async_copy(a, b, sem.at[i])
+        for i, (a, b) in enumerate(((nf, nf_out), (ns, ns_out), (tr, tr_out)))
+    ]
+    for c in copies:
+        c.start()
     for t in range(NT):
-        pltpu.make_async_copy(out.at[t], out_hbm.at[t], out_s.at[t]).wait()
-    for c in outs:
+        for h in range(2):
+            new[t, h] = all_w[t, h] - scale[t : t + 1] * all_u[t, h]
+            copies.append(pltpu.make_async_copy(new.at[t, h], new_out.at[t, h], sem_new.at[t, h]))
+            copies[-1].start()
+    for c in copies:
         c.wait()
 
 
@@ -249,43 +298,63 @@
     dma = pltpu.SemaphoreType.DMA
     any_space = pl.BlockSpec(memory_space=pl.ANY)
     smem = pl.BlockSpec(memory_space=pltpu.SMEM)
-    out, nf, ns, tr = pl.pallas_call(
+    arrays = pl.pallas_call(
         kernel,
         out_shape=(
             jax.ShapeDtypeStruct(tiles, F32),
+            jax.ShapeDtypeStruct(tiles, F32),
+            jax.ShapeDtypeStruct((8, 128), F32),
             jax.ShapeDtypeStruct(mine, F32),
             jax.ShapeDtypeStruct(mine, F32),
             jax.ShapeDtypeStruct((NT,), F32),
         ),
-        in_specs=[any_space] * 4 + [smem] * 2,
-        out_specs=(any_space, any_space, any_space, smem),
+        in_specs=[any_space] * 6,
+        out_specs=(*[any_space] * 5, smem),
         scratch_shapes=[
             pltpu.VMEM(tiles, F32),
             *[pltpu.VMEM(mine, F32)] * 5,
-            pltpu.VMEM((NT, 2, 2, 4, SIDE, 8, 128), F32),
+            *[pltpu.SMEM((NT,), F32)] * 2,
+            pltpu.VMEM((NT, 2, SIDE, SIDE, 8, 128), F32),
             pltpu.VMEM((NT, 2, SIDE, 8, 128), F32),
             pltpu.VMEM((NT, 2, SIDE, 8, 128), F32),
             pltpu.VMEM((NT, 2, SIDE, 8, 128), F32),
             pltpu.VMEM((2, SIDE, NT, 8, 128), F32),
-            pltpu.VMEM(tiles, F32),
+            pltpu.VMEM((NT, 2, SIDE, 8, 128), F32),
+            pltpu.VMEM((8, 128), F32),
             *[pltpu.VMEM((SIDE, 8, 128), F32)] * 3,
             pltpu.VMEM((3, 8, 128), F32),
-            dma((NT, 2)), dma((3,)),
-            dma, dma((NT, 2, 2, 4)),
+            dma((NT, 2)), dma((5,)),
+            dma, dma((NT, 2, SIDE)),
             dma, dma((NT, 2)),
             dma, dma((NT, 2)),
             dma, dma((2, 2, 4)),
             dma, dma((3,)),
-            dma, dma((NT, 2, 2, 4)),
-            dma((NT + 2,)),
+            dma, dma((NT, 2, SIDE)),
+            dma, dma((NT, 2, SIDE)),
+            dma((2, NT, 2)), dma((3,)),
         ],
         compiler_params=pltpu.CompilerParams(
-            collective_id=0, has_side_effects=True, vmem_limit_bytes=48 * 2**20
+            collective_id=0, has_side_effects=True, vmem_limit_bytes=24 * 2**20
         ),
         name="lamb",
     )(
-        g, *(a.reshape(mine) for a in (weights, first_moment, second_moment)), learn_rate, weight_decay
+        *(
+            pltpu.with_memory_space_constraint(a, pltpu.HBM)
+            for a in (
+                g, *(a.reshape(mine) for a in (weights, first_moment, second_moment)), learn_rate, weight_decay
+            )
+        )
     )
+    vmem = pl.BlockSpec(memory_space=pltpu.VMEM)
+    out, nf, ns, tr = pl.pallas_call(
+        results,
+        out_shape=tuple(jax.ShapeDtypeStruct(a.shape, F32) for a in (arrays[0], *arrays[3:])),
+        in_specs=[vmem] * 3 + [any_space] * 3,
+        out_specs=(any_space,) * 4,
+        scratch_shapes=[pltpu.VMEM(tiles, F32), dma((3,)), dma((NT, 2))],
+        compiler_params=pltpu.CompilerParams(vmem_limit_bytes=8 * 2**20),
+        name="results",
+    )(*(pltpu.with_memory_space_constraint(a, pltpu.VMEM) for a in arrays))
     new_weights = out.transpose(0, 1, 4, 2, 3, 5).reshape(NT, 16, SIDE * SIDE * 128)
     return new_weights, nf.reshape(NT, 16, 128), ns.reshape(NT, 16, 128), tr
 

time: 75.6 us -> 61.4 us (0.81)
  the two profiles are of different devices: /device:TPU:2 before, /device:TPU:1 now
where the time goes in v2:
time: 61.4 us; the launch traced here: 61.2 us
  Pallas kernels  60.5 us (99%)
  between operations  0.64 us (1%)
    pallas_call x1, Pallas kernels, shards(): pl.pallas_call(kernel, out_shape=(jax.ShapeDtypeStruct(tiles, F32), jax.S...  59.1 us
    pallas_call x1, Pallas kernels, shards(): pl.pallas_call(results, out_shape=tuple((jax.ShapeDtypeStruct(a.shape, F3...  1.43 us

profile of v2, /device:TPU:1, one launch (start us, length us, event | category | flops | bytes accessed | tf_op | source)
XLA Modules:
  0.0 61.2 jit_solution(8112882347794083356)
XLA Ops:
  0.6 59.1 %lamb.1 = (f32[4,2,8,8,8,128]{5,4,3,2,1,0:T(8,128)S(1)}, f32[4,2,8,8,8,128]{5,4,3,2,1,0:T(8,128)S(1)}, f32[8,128]{1,0:T(8,128)S(1)}, f32[4,2,8,128]{3,2,1,0:T(8,...) custom-call(f32[4,2,8,8,8,128]{5,4,3,2,1,0:T(8,128)} %bitcast.11, f32[4,2,8,128]{3,2,1,0:T(8,128)} %bitcast.12, ...), custom_call_target="tpu_custom_call" | custom-call | tf_op jit(solution)/shard_map/lamb/pallas_call | solution.py:301
  59.7 1.4 %results.1 = (f32[4,2,8,8,8,128]{5,4,3,2,1,0:T(8,128)}, f32[4,2,8,128]{3,2,1,0:T(8,128)}, f32[4,2,8,128]{3,2,1,0:T(8,128)}, f32[4]{0:T(128)}) custom-call(f32[4,2,8,8,8,128]{5,4,3,2,1,0:T(8,128)S(1)} %get-tuple-element.14.all_w, f32[4,2,8,8,8,128]{5,4,3,2,1,0:T(8,128)S(1)} %get-tuple-element.15.all_u, f32[8,128]{1,0:T(8,128)S(1)} %get-tuple-element.16.scale, ...), custom_call_target="tpu_custom_call" | custom-call | tf_op jit(solution)/shard_map/results/pallas_call | solution.py:349

commit v3 on v0

v3 whole, which is shorter than its diff:
```python
import functools

import jax
import jax.numpy as jnp
from jax import lax
from jax.experimental import pallas as pl
from jax.experimental.pallas import tpu as pltpu
from jax.sharding import PartitionSpec as P

STEP = 10
GROUPS = ((0, 1), (1, 2), (2, 3), (3, 4))
FAR_FIRST = (4, 3, 5, 2, 6, 1, 7)
NT = 4
SIDE = 8
F32 = jnp.float32
MESH = pl.DeviceIdType.MESH


TO_RING = ((1, 4, 3), (1, -3, -2), (2, 3, 2), (2, -2, -1), (3, 2, 1), (3, -1, 0), (4, 1, 0))
FROM_RING = ((1, 0, 1), (1, 0, -1), (2, 1, 2), (2, -1, -2), (3, 2, 3), (3, -2, -3), (4, 3, 4))
TO_SHORT = ((1, 4, 3), (1, 2, 1), (1, -3, -2), (2, 3, 1), (2, -2, -1), (3, 1, 0), (3, -1, 0))
FROM_SHORT = ((1, 0, 1), (1, 0, -1), (2, 1, 3), (2, 1, 2), (2, -1, -2), (3, 3, 4), (3, -2, -3))
TREES = ((TO_SHORT, FROM_RING, True), (TO_RING, FROM_RING, False))
WEIGHTS_AT = (((1,), (2,), (), (3,), (), ()), ((1,), (2,), (), (3,), (4,), ()))


def order(core):
    every, groups = range(NT), range(len(GROUPS))
    last_in, last_out = (tree[-1][0] for tree in TREES[core][:2])
    late = TREES[core][2]

    def weights(i):
        return [("weights", t, s) for s in WEIGHTS_AT[core][i] if s < last_out + (not late) for t in every]

    steps = [("near_weights", 1)]
    for s in range(1, last_in + 1):
        steps += [("reduce", t, s) for t in every] + [("near_weights", s + 1)] * (s < 4)
    steps += [("spread", i) for i in groups] + [("near_weights", 5)] + weights(0)
    steps += [("update", i) for i in groups] + weights(1)
    for i in groups:
        steps += [("near_updates", i)]
        for t in range(*GROUPS[i]):
            steps += [("updates", t, 1), ("squares", t)]
    steps += [("total", 0)] + weights(2)
    steps += [("updates", t, 2) for t in every] + weights(3) + [("total", 1), ("total", 2)]
    for s in range(3, last_out + (not late)):
        steps += [("updates", t, s) for t in every] + weights(s + 1)
    steps += [("total", 3)]
    if late:
        steps += [("late", t) for t in every]
    return steps + [("last", t) for t in every]


def side(t, h):
    return 1 if (t + h) % 2 == 0 else -1


def length(t, h, d):
    return 4 if (t + h + d) % 2 == 0 else 3


def kernel(
    g_hbm, w_hbm, m_hbm, v_hbm, lr_hbm, wd_hbm,
    all_w, all_u, scale_out, nf_out, ns_out, tr_out,
    g, w, m, v, nf, ns, lr, wd, ring, own, cross, u1, w1, passed, scale, sq_a, sq_b, sq_c, sq_x, squares,
    load_g, load_s, ring_s, ring_r, cross_s, cross_r, u1_s, u1_r, w1_s, w1_r, sq_s, sq_r, aw_s, aw_r, au_s, au_r, res_s, entered,
):
    dp, mp = lax.axis_index("dp"), lax.axis_index("mp")
    z, y = dp // SIDE, dp % SIDE

    def mod(i):
        return lax.rem(i + 2 * SIDE, SIDE)

    def ring_peer(h, k):
        return (z * SIDE + mod(y + k), mp) if h == 0 else (mod(z + k) * SIDE + y, mp)

    def cross_peer(h, k):
        return ring_peer(1 - h, k)

    def ring_at(h):
        return y if h == 0 else z

    def cross_at(h):
        return z if h == 0 else y

    def chunk(ref, t, h, r):
        return ref.at[t, 0, :, r] if h == 0 else ref.at[t, 1, r]

    def tile(ref, t, h, r, c):
        return ref.at[t, 0, c, r] if h == 0 else ref.at[t, 1, r, c]

    def send(src, dst, ss, rs, to):
        copy = pltpu.make_async_remote_copy(
            src_ref=src, dst_ref=dst, send_sem=ss, recv_sem=rs, device_id=to, device_id_type=MESH
        )
        copy.start()

    def arrived(ref, sem):
        pltpu.make_async_copy(ref, ref, sem).wait()

    small = [
        pltpu.make_async_copy(a, b, load_s.at[i])
        for i, (a, b) in enumerate(((w_hbm, w), (m_hbm, m), (v_hbm, v), (lr_hbm, lr), (wd_hbm, wd)))
    ]
    loads = [pltpu.make_async_copy(g_hbm.at[t, h], g.at[t, h], load_g.at[t, h]) for t in range(NT) for h in range(2)]
    for c in small + loads:
        c.start()

    other_core, along_x = (dp, mp + 1 - 2 * (mp % 2)), [(dp, mod(mp + k)) for k in (2, -2)]
    barrier = pltpu.get_barrier_semaphore()
    near = [ring_peer(h, k) for h in range(2) for k in (1, -1)]
    near += [other_core] + along_x
    for peer in near:
        pl.semaphore_signal(barrier, inc=1, device_id=peer, device_id_type=MESH)
    pl.semaphore_wait(barrier, len(near))
    for peer in along_x:
        pl.semaphore_signal(entered, inc=1, device_id=peer, device_id_type=MESH)

    first_fix = 1.0 - 0.9**STEP
    second_fix = 1.0 - 0.999**STEP
    def both_halves(core):
        held, seen = [], set()
        to_owner, from_owner, has_late = TREES[core]
        late_step = from_owner[-1][0] + (not has_late)

        def keep(src, dst, sem):
            held.append(pltpu.make_async_copy(src, dst, sem))
            held[-1].start()

        def block_sum(t, h, at, s):
            mine = chunk(g_hbm if s == 1 else g, t, h, mod(ring_at(h) - side(t, h) * at))
            parts = [ring.at[t, h, a % SIDE] for _, a, b in to_owner if b == at]
            for _, a, b in to_owner:
                if b == at:
                    arrived(ring.at[t, h, a % SIDE], ring_r.at[t, h, a % SIDE])
            return mine, parts

        def reduce(t, s):
            for h in range(2):
                if s == 2:
                    loads[2 * t + h].wait()
                for step, a, b in to_owner:
                    if step == s:
                        src, parts = block_sum(t, h, a, s)
                        if parts:
                            total = src[...]
                            for part in parts:
                                total += part[...]
                            src = parts[0]
                            src[...] = total
                        send(
                            src, ring.at[t, h, a % SIDE], ring_s, ring_r.at[t, h, a % SIDE],
                            ring_peer(h, side(t, h) * (b - a)),
                        )

        def near_weights(s):
            if s == 1:
                for c in small:
                    c.wait()
                for h in range(2):
                    w1[h, cross_at(h)] = w[:, h]
            for h in range(2):
                for d, sign in enumerate((1, -1)):
                    n = length(0, h, d)
                    if 1 < s <= n + 1:
                        at = w1.at[h, mod(cross_at(h) - sign * (s - 1))]
                        arrived(at, w1_r.at[h, d, s - 2])
                    if s <= n:
                        at = w1.at[h, mod(cross_at(h) - sign * (s - 1))]
                        send(at, at, w1_s, w1_r.at[h, d, s - 1], cross_peer(h, sign))

        def across(src, dst, i, ss, rs):
            lo, hi = GROUPS[i]
            for k in FAR_FIRST:
                for h in range(2):
                    at = cross_at(h) if src is u1 else mod(cross_at(h) + k)
                    send(src.at[h, at, lo:hi], dst.at[h, cross_at(h), lo:hi], ss, rs.at[i, h], cross_peer(h, k))

        def came_across(dst, i, rs):
            lo, hi = GROUPS[i]
            for h in range(2):
                arrived(dst.at[h, 0:7, lo:hi], rs.at[i, h])

        def spread(i):
            for t in range(*GROUPS[i]):
                for h in range(2):
                    src, parts = block_sum(t, h, 0, 5)
                    total = src[...]
                    for part in parts:
                        total += part[...]
                    own[h, :, t] = total
            across(own, cross, i, cross_s, cross_r)

        def update(i):
            lo, hi = GROUPS[i]
            for h in range(2):
                cross[h, cross_at(h), lo:hi] = own[h, cross_at(h), lo:hi]
            came_across(cross, i, cross_r)
            for h in range(2):
                summed = jnp.sum(cross[h, :, lo:hi], axis=0) * (1.0 / (SIDE * SIDE))
                new_first = 0.9 * m[lo:hi, h] + 0.1 * summed
                new_second = 0.999 * v[lo:hi, h] + 0.001 * summed * summed
                nf[lo:hi, h] = new_first
                ns[lo:hi, h] = new_second
                part = new_first / first_fix / (jnp.sqrt(new_second / second_fix) + 1e-06)
                for t in range(lo, hi):
                    u1[h, cross_at(h), t] = part[t - lo] + wd[t] * w[t, h]
            across(u1, u1, i, u1_s, u1_r)

        def squared(a):
            return jnp.sum(jnp.sum(a * a, axis=0), axis=0, keepdims=True)

        def near_updates(i):
            came_across(u1, i, u1_r)

        def squares_of(t):
            for h in range(2):
                squares[h, t : t + 1] = squared(w1[h, :, t])
                squares[h, NT + t : NT + t + 1] = squared(u1[h, :, t])

        def total(stage):
            if stage == 0:
                for h, slots in enumerate((sq_a, sq_b)):
                    slots[ring_at(h)] = squares[h]
                    for k in FAR_FIRST:
                        send(squares.at[h], slots.at[ring_at(h)], sq_s, sq_r.at[h], ring_peer(h, k))
            if stage == 1:
                for h, slots in enumerate((sq_a, sq_b)):
                    arrived(slots.at[0:7], sq_r.at[h])
                squares[2] = jnp.sum(sq_a[...], axis=0) + jnp.sum(sq_b[...], axis=0)
                sq_c[mp % 2] = squares[2]
                send(squares.at[2], sq_c.at[mp % 2], sq_s, sq_r.at[2], other_core)
            if stage == 2:
                arrived(sq_c.at[0], sq_r.at[2])
                squares[3] = sq_c[0] + sq_c[1]
                sq_x[mp // 2] = squares[3]
                pl.semaphore_wait(entered, 2)
                for k in (4, 2, 6):
                    send(squares.at[3], sq_x.at[mp // 2], sq_s, sq_r.at[3], (dp, mod(mp + k)))
            if stage == 3:
                arrived(sq_x.at[0:3], sq_r.at[3])
                both = jnp.sum(sq_x[...], axis=0)
                roots = jnp.sqrt(jnp.sum(both, axis=1, keepdims=True))
                ratio = roots[0:NT] / (roots[NT:] + 1e-06)
                for t in range(NT):
                    tr_out[t] = jnp.max(ratio[t : t + 1])
                    scale[t : t + 1] = jnp.broadcast_to(lr[t] * ratio[t : t + 1], (1, 128))
                keep(scale, scale_out, res_s.at[2])

        def around(first, ref, t, s, sems, sem):
            for h in range(2):
                for step, a, b in from_owner:
                    if step == s < late_step:
                        at = chunk(ref, t, h, place(t, h, a))
                        if a:
                            landed(ref, t, h, a, sems)
                        send(
                            at if a else first.at[h, :, t], at, sem, sems.at[t, h, b % SIDE],
                            ring_peer(h, side(t, h) * (b - a)),
                        )

        def place(t, h, a):
            return mod(ring_at(h) - side(t, h) * a)

        def landed(ref, t, h, a, sems):
            if (ref is all_w, t, h, a) not in seen:
                seen.add((ref is all_w, t, h, a))
                arrived(chunk(ref, t, h, place(t, h, a)), sems.at[t, h, a % SIDE])

        def late(t):
            for h in range(2):
                for step, a, b in from_owner:
                    if step == late_step:
                        landed(all_w, t, h, a, aw_r)
                        landed(all_u, t, h, a, au_r)
                        at = chunk(all_w, t, h, place(t, h, a))
                        new = passed.at[t, h, a % 2]
                        new[...] = at[...] - scale[t : t + 1] * chunk(all_u, t, h, place(t, h, a))[...]
                        send(new, at, aw_s, aw_r.at[t, h, b % SIDE], ring_peer(h, side(t, h) * (b - a)))

        def last(t):
            for h in range(2):
                for step, _, a in from_owner:
                    landed(all_w, t, h, a, aw_r)
                    if step < late_step:
                        landed(all_u, t, h, a, au_r)

        def weights(t, s):
            if s == 1:
                for h in range(2):
                    chunk(all_w, t, h, ring_at(h))[...] = w1[h, :, t]
                    for step, _, a in from_owner:
                        if step == late_step:
                            chunk(all_u, t, h, place(t, h, a))[...] = jnp.zeros((SIDE, 8, 128), F32)
            around(w1, all_w, t, s, aw_r, aw_s)

        def updates(t, s):
            around(u1, all_u, t, s, au_r, au_s)
            if s == 1:
                for h in range(2):
                    chunk(all_u, t, h, ring_at(h))[...] = u1[h, :, t]

        acts = {
            "reduce": reduce, "near_weights": near_weights, "spread": spread, "update": update,
            "near_updates": near_updates, "squares": squares_of, "total": total, "weights": weights, "updates": updates, "late": late, "last": last,
        }
        for name, *args in order(core):
            acts[name](*args)
            if name == "update" and args[0] == len(GROUPS) - 1:
                keep(nf, nf_out, res_s.at[0])
                keep(ns, ns_out, res_s.at[1])

        arrived(g.at[:, :, 0:7], ring_s)
        arrived(g.at[:, :, 0:7], aw_s)
        arrived(g.at[:, :, 0 : sum(step < late_step for step, _, _ in from_owner)], au_s)
        arrived(g.at[0, 0, 0:7], cross_s)
        arrived(g.at[0, 0, 0:7], u1_s)
        arrived(g.at[0, 0, 0:7], w1_s)
        arrived(g.at[0, 0:1, 0:3, 0:6], sq_s)
        for c in held:
            c.wait()

    for core in range(2):

        @pl.when(mp % 2 == core)
        def _(core=core):
            both_halves(core)


def results(all_w, all_u, scale, nf, ns, tr, new_out, nf_out, ns_out, tr_out, new, sem, sem_new):
    copies = [
        pltpu.make_async_copy(a, b, sem.at[i])
        for i, (a, b) in enumerate(((nf, nf_out), (ns, ns_out), (tr, tr_out)))
    ]
    for c in copies:
        c.start()
    for t in range(NT):
        for h in range(2):
            new[t, h] = all_w[t, h] - scale[t : t + 1] * all_u[t, h]
            copies.append(pltpu.make_async_copy(new.at[t, h], new_out.at[t, h], sem_new.at[t, h]))
            copies[-1].start()
    for c in copies:
        c.wait()


def shards(gradients, weights, first_moment, second_moment, learn_rate, weight_decay):
    tiles = (NT, 2, SIDE, SIDE, 8, 128)
    mine = (NT, 2, 8, 128)
    g = gradients.reshape(NT, 2, 8, SIDE, SIDE, 128).transpose(0, 1, 3, 4, 2, 5)
    dma = pltpu.SemaphoreType.DMA
    any_space = pl.BlockSpec(memory_space=pl.ANY)
    smem = pl.BlockSpec(memory_space=pltpu.SMEM)
    vmem = pl.BlockSpec(memory_space=pltpu.VMEM)
    arrays = pl.pallas_call(
        kernel,
        out_shape=(
            jax.ShapeDtypeStruct(tiles, F32),
            jax.ShapeDtypeStruct(tiles, F32),
            jax.ShapeDtypeStruct((8, 128), F32),
            jax.ShapeDtypeStruct(mine, F32),
            jax.ShapeDtypeStruct(mine, F32),
            jax.ShapeDtypeStruct((NT,), F32),
        ),
        in_specs=[any_space] * 6,
        out_specs=(vmem, vmem, *[any_space] * 3, smem),
        scratch_shapes=[
            pltpu.VMEM(tiles, F32),
            *[pltpu.VMEM(mine, F32)] * 5,
            *[pltpu.SMEM((NT,), F32)] * 2,
            pltpu.VMEM((NT, 2, SIDE, SIDE, 8, 128), F32),
            *[pltpu.VMEM((2, SIDE, NT, 8, 128), F32)] * 4,
            pltpu.VMEM((NT, 2, 2, SIDE, 8, 128), F32),
            pltpu.VMEM((8, 128), F32),
            *[pltpu.VMEM((SIDE, 8, 128), F32)] * 2,
            pltpu.VMEM((2, 8, 128), F32),
            pltpu.VMEM((4, 8, 128), F32),
            pltpu.VMEM((4, 8, 128), F32),
            dma((NT, 2)), dma((5,)),
            dma, dma((NT, 2, SIDE)),
            dma, dma((len(GROUPS), 2)),
            dma, dma((len(GROUPS), 2)),
            dma, dma((2, 2, 4)),
            dma, dma((4,)),
            dma, dma((NT, 2, SIDE)),
            dma, dma((NT, 2, SIDE)),
            dma((3,)),
            pltpu.SemaphoreType.REGULAR,
        ],
        compiler_params=pltpu.CompilerParams(
            collective_id=0, has_side_effects=True, vmem_limit_bytes=24 * 2**20
        ),
        name="lamb",
    )(
        *(
            pltpu.with_memory_space_constraint(a, pltpu.HBM)
            for a in (
                g, *(a.reshape(mine) for a in (weights, first_moment, second_moment)), learn_rate, weight_decay
            )
        )
    )
    out, nf, ns, tr = pl.pallas_call(
        results,
        out_shape=tuple(jax.ShapeDtypeStruct(a.shape, F32) for a in (arrays[0], *arrays[3:])),
        in_specs=[vmem] * 3 + [any_space] * 3,
        out_specs=(any_space,) * 4,
        scratch_shapes=[pltpu.VMEM(tiles, F32), dma((3,)), dma((NT, 2))],
        compiler_params=pltpu.CompilerParams(vmem_limit_bytes=8 * 2**20),
        name="results",
    )(*(pltpu.with_memory_space_constraint(a, pltpu.VMEM) for a in arrays))
    new_weights = out.transpose(0, 1, 4, 2, 3, 5).reshape(NT, 16, SIDE * SIDE * 128)
    return new_weights, nf.reshape(NT, 16, 128), ns.reshape(NT, 16, 128), tr


def solution(mesh):
    in_specs = (
        P("dp", None, "mp", None),
        P(None, "mp", "dp"),
        P(None, "mp", "dp"),
        P(None, "mp", "dp"),
        P(),
        P(),
    )
    out_specs = (P(None, "mp", None), P(None, "mp", "dp"), P(None, "mp", "dp"), P())
    return jax.shard_map(shards, mesh=mesh, in_specs=in_specs, out_specs=out_specs, check_vma=False)
```

time: 194 us -> 60.3 us (0.31)
  waiting for transfers between devices: 87.5 us -> 0 us
  blocking collectives: 80.2 us -> 0 us
  Pallas kernels: 0 us -> 59.6 us
  between operations: 14.1 us -> 0.64 us
  other arithmetic: 8.58 us -> 0 us
  local copies, waits for them, and re-layouts: 3.84 us -> 0 us
    all_gather x1 -> x0, waiting for transfers between devices: 87.5 us -> none  [in_one_piece(): lax.all_gather(both, axis, axis=dim, tiled=True)]
    all_to_all x2 -> x0, blocking collectives: 80.2 us -> none  [the longest x1 66.2 us: sent_and_summed(): lax.all_to_all(parts, axis, split_axis=0, concat_axis=0, tiled=True)]
    pallas_call x0 -> x2, Pallas kernels: none -> 59.6 us  [the longest x1 58.2 us: shards(): pl.pallas_call(kernel, out_shape=(jax.ShapeDtypeStruct(tiles, F32), jax.S...]
    sub x1 -> x0, other arithmetic: 3.81 us -> none  [shards(): whole_weights - (learn_rate * trust_ratio)[:, None, None] * whole_update]
    reduce_sum x3 -> x0, other arithmetic: 2.82 us -> none  [the longest x1 2.66 us: shards(): jnp.sum(whole_weights * whole_weights, axis=(1, 2))]
    unnamed x11 -> x0, local copies, waits for them, and re-layouts: 2.62 us -> none
  transfers between devices with their start and end apart: 1 -> 0, of which waited for: 1 -> 0; matrix products, arithmetic and copies ran while one was open for 0% -> 0% of each run, Pallas kernels for 0% -> 0%
where the time goes in v3:
time: 60.3 us; the launch traced here: 60.2 us
  Pallas kernels  59.6 us (99%)
  between operations  0.64 us (1%)
    pallas_call x1, Pallas kernels, shards(): pl.pallas_call(kernel, out_shape=(jax.ShapeDtypeStruct(tiles, F32), jax.S...  58.2 us
    pallas_call x1, Pallas kernels, shards(): pl.pallas_call(results, out_shape=tuple((jax.ShapeDtypeStruct(a.shape, F3...  1.43 us

profile of v3, /device:TPU:1, one launch (start us, length us, event | category | flops | bytes accessed | tf_op | source)
XLA Modules:
  0.0 60.2 jit_solution(16510033154027065837)
XLA Ops:
  0.6 58.2 %lamb.1 = (f32[4,2,8,8,8,128]{5,4,3,2,1,0:T(8,128)S(1)}, f32[4,2,8,8,8,128]{5,4,3,2,1,0:T(8,128)S(1)}, f32[8,128]{1,0:T(8,128)S(1)}, f32[4,2,8,128]{3,2,1,0:T(8,...) custom-call(f32[4,2,8,8,8,128]{5,4,3,2,1,0:T(8,128)} %bitcast.11, f32[4,2,8,128]{3,2,1,0:T(8,128)} %bitcast.12, ...), custom_call_target="tpu_custom_call" | custom-call | tf_op jit(solution)/shard_map/lamb/pallas_call | solution.py:354
  58.8 1.4 %results.1 = (f32[4,2,8,8,8,128]{5,4,3,2,1,0:T(8,128)}, f32[4,2,8,128]{3,2,1,0:T(8,128)}, f32[4,2,8,128]{3,2,1,0:T(8,128)}, f32[4]{0:T(128)}) custom-call(f32[4,2,8,8,8,128]{5,4,3,2,1,0:T(8,128)S(1)} %get-tuple-element.14.all_w, f32[4,2,8,8,8,128]{5,4,3,2,1,0:T(8,128)S(1)} %get-tuple-element.15.all_u, f32[8,128]{1,0:T(8,128)S(1)} %get-tuple-element.16.scale, ...), custom_call_target="tpu_custom_call" | custom-call | tf_op jit(solution)/shard_map/results/pallas_call | solution.py:401

commit v4 on v3

--- a/solution.py
+++ b/solution.py
@@ -103,7 +103,7 @@
         for i, (a, b) in enumerate(((w_hbm, w), (m_hbm, m), (v_hbm, v), (lr_hbm, lr), (wd_hbm, wd)))
     ]
     loads = [pltpu.make_async_copy(g_hbm.at[t, h], g.at[t, h], load_g.at[t, h]) for t in range(NT) for h in range(2)]
-    for c in small + loads:
+    for c in small[:1] + loads + small[1:]:
         c.start()
 
     other_core, along_x = (dp, mp + 1 - 2 * (mp % 2)), [(dp, mod(mp + k)) for k in (2, -2)]
@@ -128,7 +128,7 @@
             held[-1].start()
 
         def block_sum(t, h, at, s):
-            mine = chunk(g_hbm if s == 1 else g, t, h, mod(ring_at(h) - side(t, h) * at))
+            mine = chunk(g, t, h, mod(ring_at(h) - side(t, h) * at))
             parts = [ring.at[t, h, a % SIDE] for _, a, b in to_owner if b == at]
             for _, a, b in to_owner:
                 if b == at:
@@ -137,7 +137,7 @@
 
         def reduce(t, s):
             for h in range(2):
-                if s == 2:
+                if s == 1:
                     loads[2 * t + h].wait()
                 for step, a, b in to_owner:
                     if step == s:

time: 60.3 us -> 60.2 us (level)
  no operation moved by 1% of the time
where the time goes in v4:
time: 60.2 us; the launch traced here: 60.1 us
  Pallas kernels  59.5 us (99%)
  between operations  0.64 us (1%)
    pallas_call x1, Pallas kernels, shards(): pl.pallas_call(kernel, out_shape=(jax.ShapeDtypeStruct(tiles, F32), jax.S...  58 us
    pallas_call x1, Pallas kernels, shards(): pl.pallas_call(results, out_shape=tuple((jax.ShapeDtypeStruct(a.shape, F3...  1.43 us

profile of v4, /device:TPU:1, one launch (start us, length us, event | category | flops | bytes accessed | tf_op | source)
XLA Modules:
  0.0 60.1 jit_solution(12946503267669163680)
XLA Ops:
  0.6 58.0 %lamb.1 = (f32[4,2,8,8,8,128]{5,4,3,2,1,0:T(8,128)S(1)}, f32[4,2,8,8,8,128]{5,4,3,2,1,0:T(8,128)S(1)}, f32[8,128]{1,0:T(8,128)S(1)}, f32[4,2,8,128]{3,2,1,0:T(8,...) custom-call(f32[4,2,8,8,8,128]{5,4,3,2,1,0:T(8,128)} %bitcast.11, f32[4,2,8,128]{3,2,1,0:T(8,128)} %bitcast.12, ...), custom_call_target="tpu_custom_call" | custom-call | tf_op jit(solution)/shard_map/lamb/pallas_call | solution.py:354
  58.7 1.4 %results.1 = (f32[4,2,8,8,8,128]{5,4,3,2,1,0:T(8,128)}, f32[4,2,8,128]{3,2,1,0:T(8,128)}, f32[4,2,8,128]{3,2,1,0:T(8,128)}, f32[4]{0:T(128)}) custom-call(f32[4,2,8,8,8,128]{5,4,3,2,1,0:T(8,128)S(1)} %get-tuple-element.14.all_w, f32[4,2,8,8,8,128]{5,4,3,2,1,0:T(8,128)S(1)} %get-tuple-element.15.all_u, f32[8,128]{1,0:T(8,128)S(1)} %get-tuple-element.16.scale, ...), custom_call_target="tpu_custom_call" | custom-call | tf_op jit(solution)/shard_map/results/pallas_call | solution.py:401
